TPU v7x, 32 devices: a whole 2x2x4 slice. The times are simulated.
32 devices in a mesh: tile: 8 (over z, y), src: 4 (over x, core).
Axes of the slice: x: 2, y: 2, z: 4, core: 2. Of those that a mesh axis runs over, the one named last changes fastest.
Arguments:
- tile_tokens: bfloat16 [8192, 2048], P(('tile', 'src')), may hold values from -6 to 6
- norm_gain: float32 [2048], replicated, may hold values from 0.25 to 2.5
- up_weight: bfloat16 [2048, 2816], P('tile'), may hold values from -0.125 to 0.125
- down_weight: bfloat16 [2816, 2048], P('tile'), may hold values from -0.109375 to 0.109375
- head_weight: bfloat16 [2048, 768], P(None, 'src'), may hold values from -0.125 to 0.125
- source_index: int32 [32, 2], replicated, may hold values from 0 to 96, as said below
- source_cutoff: int32 [32], replicated, may hold values from 8 to 16
- source_weight: float32 [32], replicated, may hold values from 0.3 to 3
Outputs:
- intensity: float32 [32, 4096], P(('tile', 'src'))
Inputs may be any that keep to these rules, and one draw needn't show every extreme that they name: `source_index`: in each aligned group of 4 source points the first has the least value of the group in both coordinates, the second lies exactly 32 beyond it in both, and every other lies within 32 of the first in both.
All inputs are finite; a program needn't handle non-finite values.
Results may differ from a plain program's by a relative error of at most 0.0007.
Values may be sent and summed in bfloat16 or wider, within the bound.
A program may use at most 128 MiB of HBM per device.

v0:
```python
import math

import jax
import jax.numpy as jnp
from jax import lax
from jax.sharding import PartitionSpec as P

GRID = 16
SUB = 8
W = 32
REG = 64
PIX = 64
SRC_DEV = 4
PATCH = 256
ORD = 128


def dft_tables():
    frequency = jnp.arange(W, dtype=jnp.int32) - W // 2
    position = jnp.arange(PIX, dtype=jnp.int32)
    phase_turns = jnp.mod(frequency[:, None] * position[None, :], PIX).astype(jnp.float32)
    phase_angle = phase_turns * (2.0 * math.pi / PIX)
    cosine = jnp.cos(phase_angle)
    sine_table = jnp.sin(phase_angle)
    table_one = jnp.concatenate(
        [jnp.concatenate([cosine, sine_table], 1), jnp.concatenate([-sine_table, cosine], 1)], 0
    )
    table_two = jnp.concatenate(
        [
            jnp.concatenate([cosine.T, -sine_table.T], 1),
            jnp.concatenate([sine_table.T, cosine.T], 1),
        ],
        0,
    )
    return (table_one, table_two)


def pupil_mask(radius):
    frequency = jnp.arange(W, dtype=jnp.int32) - W // 2
    distance = frequency[:, None] * frequency[:, None] + frequency[None, :] * frequency[None, :]
    return (distance <= radius * radius).astype(jnp.bfloat16)


def source_power(window, table_one, table_two):
    tile_count = window.shape[0]
    split_parts = (
        window.reshape(tile_count, 6, 2, W, W)
        .transpose(0, 1, 3, 2, 4)
        .reshape(tile_count, 6, W, 2 * W)
    )
    half_field = jnp.einsum(
        "bcik,ky->bciy", split_parts.astype(jnp.float32), table_one, precision=lax.Precision.HIGHEST
    )
    half_field = (
        half_field.reshape(tile_count, 6, W, 2, PIX)
        .transpose(0, 1, 3, 2, 4)
        .reshape(tile_count, 6, 2 * W, PIX)
    )
    image_field = jnp.einsum(
        "pk,bcky->bcpy", table_two, half_field, precision=lax.Precision.HIGHEST
    )
    power_map = jnp.sum((image_field * image_field).reshape(tile_count, 12, PIX, PIX), axis=1)
    return power_map.reshape(tile_count, PIX * PIX)


def local(
    tile_tokens,
    norm_gain,
    up_weight,
    down_weight,
    head_weight,
    source_index,
    source_cutoff,
    source_weight,
):
    residual = tile_tokens.astype(jnp.float32)
    mean_square = jnp.mean(residual * residual, axis=1, keepdims=True)
    normed = (residual * lax.rsqrt(mean_square + 1e-05) * norm_gain).astype(jnp.bfloat16)
    token_count = tile_tokens.shape[0]
    columns = normed
    pre_act = jnp.dot(
        columns,
        lax.all_gather(up_weight, "tile", axis=0, tiled=True),
        preferred_element_type=jnp.float32,
    )
    hidden = jax.nn.gelu(pre_act).astype(jnp.bfloat16)
    columns = hidden
    branch_out = jnp.dot(
        columns,
        lax.all_gather(down_weight, "tile", axis=0, tiled=True),
        preferred_element_type=jnp.float32,
    )
    mixed = (residual + branch_out).astype(jnp.bfloat16)
    coeffs = jnp.dot(
        mixed,
        lax.all_gather(head_weight, "src", axis=1, tiled=True),
        preferred_element_type=jnp.float32,
    ).astype(jnp.bfloat16)
    tile_count = token_count // PATCH
    spectra = (
        coeffs.reshape(tile_count, GRID, GRID, 12, SUB, SUB)
        .transpose(0, 3, 1, 4, 2, 5)
        .reshape(tile_count, 12, ORD, ORD)
    )
    group_count = lax.axis_size("tile")
    my_group = lax.axis_index("tile")
    anchor_zero = jnp.zeros((), jnp.int32)
    local_weight = lax.dynamic_slice_in_dim(source_weight, my_group * SRC_DEV, SRC_DEV, 0)
    table_one, table_two = dft_tables()
    image_count = group_count * tile_count
    running = jnp.zeros((image_count, PIX * PIX), jnp.float32)
    corner = jnp.min(source_index.reshape(group_count, SRC_DEV, 2), axis=1)

    def cut_region(corner_at):
        return lax.dynamic_slice(
            spectra,
            (anchor_zero, anchor_zero, corner_at[0], corner_at[1]),
            (tile_count, 12, REG, REG),
        )

    cut_blocks = jax.vmap(cut_region)(corner).reshape(group_count, tile_count, 12, REG * REG)
    received = lax.all_to_all(cut_blocks, "tile", split_axis=0, concat_axis=1, tiled=True)
    region = received.reshape(image_count, 12, REG, REG)
    base_corner = lax.dynamic_index_in_dim(corner, my_group, 0, keepdims=False)
    local_index = (
        lax.dynamic_slice_in_dim(source_index, my_group * SRC_DEV, SRC_DEV, 0)
        - base_corner[None, :]
    )
    local_cutoff = lax.dynamic_slice_in_dim(source_cutoff, my_group * SRC_DEV, SRC_DEV, 0)

    def add_source(total, source_item):
        corner_at, radius, weight = source_item
        window = lax.dynamic_slice(
            region, (anchor_zero, anchor_zero, corner_at[0], corner_at[1]), (image_count, 12, W, W)
        ) * pupil_mask(radius)
        return (total + weight * source_power(window, table_one, table_two), None)

    image_sum, unused = lax.scan(add_source, running, (local_index, local_cutoff, local_weight))
    norm_scale = 1.0 / (6.0 * W * W * source_weight.shape[0])
    everything = lax.psum(image_sum, "tile")
    result = lax.dynamic_slice_in_dim(everything, my_group * tile_count, tile_count, 0)
    return result * norm_scale


def solution(mesh):
    return jax.shard_map(
        local,
        mesh=mesh,
        in_specs=(
            P(("tile", "src"), None),
            P(),
            P("tile", None),
            P("tile", None),
            P(None, "src"),
            P(),
            P(),
            P(),
        ),
        out_specs=P(("tile", "src"), None),
        check_vma=False,
    )
```

profile of v0, /device:TPU:1, one launch (start us, length us, event | category | flops | bytes accessed | tf_op | source)
XLA Modules:
  0.0 593.2 jit_solution(10851161338368518987)
XLA Ops:
  9.4 165.5 %all-gather.4.cloned.1.call-done = bf16[2048,2816]{1,0:T(8,128)(2,1)} async-done(((bf16[256,2816]{1,0:T(8,128)(2,1)}), bf16[2048,2816]{1,0:T(8,128)(2,1)}) %all-gather.4.cloned.1.call-update) | async-done | bytes 11534352 | tf_op jit(solution)/shard_map/all_gather | solution.py:83
  174.9 164.0 %all-gather.6.cloned.1.call-done = bf16[2816,2048]{1,0:T(8,128)(2,1)} async-done(((bf16[352,2048]{1,0:T(8,128)(2,1)}), bf16[2816,2048]{1,0:T(8,128)(2,1)}) %all-gather.6.cloned.1.call-update) | async-done | bytes 11534352 | tf_op jit(solution)/shard_map/all_gather | solution.py:90
  339.0 14.1 %fusion.13 = bf16[256,2048]{1,0:T(8,128)(2,1)S(1)} fusion(bf16[2816,2048]{1,0:T(8,128)(2,1)} %all-gather.6.cloned.1.call-done, bf16[256,2048]{1,0:T(8,128)(2,1)S(1)} %copy-done.2, bf16[2048,2816]{1,0:T(8,128)(2,1)} %all-gather.4.cloned.1.call-done, f32[2048]{0:T(1024)S(1)} %copy-done.4, f32[256]{0:T(256)S(1)} %add_rsqrt_fusion), kind=kOutput, calls=%fused_computation.26 | convolution fusion | flops 5915738112 | bytes 25175040 | tf_op jit(solution)/shard_map/dot_general | solution.py:88
  353.0 15.0 %all-gather.8.cloned.1.call-done = bf16[2048,768]{0,1:T(8,128)(2,1)} async-done(((bf16[2048,192]{0,1:T(8,128)(2,1)}), bf16[2048,768]{0,1:T(8,128)(2,1)}) %all-gather.8.cloned.1.call-update) | async-done | bytes 3145744 | tf_op jit(solution)/shard_map/all_gather | solution.py:96
  368.1 2.9 convolution_convert_fusion
  371.2 2.1 reshape.116
  373.3 5.4 copy.23
  378.7 8.3 %reshape.117 = bf16[1,12,128,128]{3,2,1,0:T(8,128)(2,1)S(1)} reshape(bf16[1,12,16,8,16,8]{5,4,3,2,1,0:T(8,128)(2,1)} %copy.23) | data formatting | bytes 786432 | tf_op jit(solution)/shard_map/reshape | solution.py:103
  387.0 16.1 %while.14 = (s32[]{:T(128)}, bf16[1,12,128,128]{3,2,1,0:T(8,128)(2,1)S(1)}, s32[8,4]{0,1:T(4,128)S(1)}, bf16[8,1,12,64,64]{4,3,2,1,0:T(8,128)(2,1)S(1)}, s32[]{:T(128)}) while((s32[]{:T(128)}, bf16[1,12,128,128]{3,2,1,0:T(8,128)(2,1)S(1)}, s32[8,4]{0,1:T(4,128)S(1)}, bf16[8,1,12,64,64]{4,3,2,1,0:T(8,128)(2,1)S(1)}, s32[]{:T(128)}) %tuple.68), condition=%wide.while_cond, body=%wide.while_body.sunk | while | flops 2 | bytes 393341 | solution.py:115
  403.2 2.2 reshape.154
  405.4 5.2 all-to-all-start
  413.1 22.9 %all-to-all-done = bf16[8,1,12,4096]{3,2,1,0:T(8,128)(2,1)S(1)} async-done(((bf16[8,1,12,4096]{3,2,1,0:T(8,128)(2,1)}), bf16[8,1,12,4096]{3,2,1,0:T(8,128)(2,1)S(1)}, u32[]{:S(2)}, u32[]{:S(2)}) %all-to-all-start) | async-done | bytes 786464 | tf_op jit(solution)/shard_map/all_to_all | solution.py:122
  436.0 2.6 reshape.155
  438.6 79.0 %while.15 = (s32[]{:T(128)}, f32[8,4096]{1,0:T(8,128)S(1)}, f32[4]{0:T(128)S(1)}, s32[4,2]{0,1:T(2,128)S(1)}, bf16[8,12,64,64]{3,2,1,0:T(8,128)(2,1)}, /*index=5...) while((s32[]{:T(128)}, f32[8,4096]{1,0:T(8,128)S(1)}, ...), condition=%wide.region_4.5_spmd.clone, body=%wide.region_2.4_spmd.clone.sunk | while | flops 454233152 | bytes 10359327 | solution.py:138
  445.2 1.8 dynamic-slice_multiply_fusion.3
  449.8 4.5 fusion.77
  454.3 2.1 copy.39
  469.5 4.5 fusion.77
  474.0 2.1 copy.39
  489.3 4.5 fusion.77
  493.8 2.1 copy.39
  509.1 4.5 fusion.77
  513.6 2.1 copy.39
  518.3 66.8 %all-reduce.2.cloned.1.call-done = f32[8,4096]{1,0:T(8,128)} async-done(((f32[8,4096]{1,0:T(8,128)}), f32[8,4096]{1,0:T(8,128)}) %all-reduce.2.cloned.1.call-update) | async-done | bytes 131088 | tf_op jit(solution)/shard_map/psum | solution.py:140
  (123 shorter events, 53.2 us)
Async XLA Ops:
  6.5 2.2 copy-start.3
  6.5 2.4 copy-start.2
  6.5 332.4 %copy-start.4 = (f32[2048]{0:T(1024)S(1)}, f32[2048]{0:T(1024)}, u32[]{:S(2)}) copy-start(f32[2048]{0:T(1024)} %param.11) | copy-start | bytes 24580
  6.5 168.4 %all-gather.4.cloned.1.call-start = ((), (), s32[]{:S(2)}) async-start(), calls=%async_computation.1 | async-start | bytes 12976128 | tf_op jit(solution)/shard_map/all_gather | solution.py:83
  7.3 331.7 %all-gather.6.cloned.1.call-start = ((), (), s32[]{:S(2)}) async-start(), calls=%async_computation.2 | async-start | bytes 12976128 | tf_op jit(solution)/shard_map/all_gather | solution.py:90
  8.0 360.1 %all-gather.8.cloned.1.call-start = ((), (), s32[]{:S(2)}) async-start(), calls=%async_computation.3 | async-start | bytes 3932160 | tf_op jit(solution)/shard_map/all_gather | solution.py:96
  378.7 8.3 %copy-start.1 = (bf16[8,1,12,64,64]{4,3,2,1,0:T(8,128)(2,1)S(1)}, bf16[8,1,12,64,64]{4,3,2,1,0:T(8,128)(2,1)}, u32[]{:S(2)}) copy-start(bf16[8,1,12,64,64]{4,3,2,1,0:T(8,128)(2,1)} %custom-call.1) | copy-start | bytes 2359300
  403.2 7.9 %copy-start.5 = (f32[32]{0:T(128)S(1)}, f32[32]{0:T(128)}, u32[]{:S(2)}) copy-start(f32[32]{0:T(128)} %param.17) | copy-start | bytes 388
  403.2 8.0 %copy-start.6 = (s32[32]{0:T(128)S(1)}, s32[32]{0:T(128)}, u32[]{:S(2)}) copy-start(s32[32]{0:T(128)} %param.16) | copy-start | bytes 388
  405.4 30.6 %all-to-all-start = ((bf16[8,1,12,4096]{3,2,1,0:T(8,128)(2,1)}), bf16[8,1,12,4096]{3,2,1,0:T(8,128)(2,1)S(1)}, u32[]{:S(2)}, u32[]{:S(2)}) async-start(bf16[8,1,12,4096]{3,2,1,0:T(8,128)(2,1)} %bitcast.21), calls=%async_computation | async-start | bytes 2097152 | tf_op jit(solution)/shard_map/all_to_all | solution.py:122
  410.7 174.4 %all-reduce.2.cloned.1.call-start = ((), (), s32[]{:S(2)}) async-start(), calls=%async_computation.4 | async-start | bytes 262144 | tf_op jit(solution)/shard_map/psum | solution.py:140
  517.6 0.6 copy-start
Sparse Core Ops, SparseCore 0:
  9.6 165.3 all-gather.3
  177.1 161.8 all-gather.5
  340.5 27.5 all-gather.7
  518.4 66.6 all-reduce.1
where the time goes:
time: 597 us; the launch traced here: 593 us
  waiting for transfers between devices  436 us (73%)
  local copies, waits for them, and re-layouts  60.1 us (10%)
  matrix products  41.7 us (7%)
  loops' own time  21.2 us (4%)
  other arithmetic  14.9 us (2%)
  between operations  13.3 us (2%)
    all_gather x1, waiting for transfers between devices, local(): lax.all_gather(up_weight, 'tile', axis=0, tiled=True)  166 us
    all_gather x1, waiting for transfers between devices, local(): lax.all_gather(down_weight, 'tile', axis=0, tiled=True)  164 us
    psum x1, waiting for transfers between devices, local(): everything = lax.psum(image_sum, 'tile')  66.8 us
    all_to_all x1, waiting for transfers between devices, local(): lax.all_to_all(cut_blocks, 'tile', split_axis=0, concat_axis=1, tiled=True)  22.9 us
    another operation x1, loops' own time, local(): lax.scan(add_source, running, (local_index, local_cutoff, local_weight))  21 us
    dot_general x4, matrix products, source_power(): jnp.einsum('pk,bcky->bcpy', table_two, half_field, precision=lax.Precisio...  18.1 us
    gather x24, local copies, waits for them, and re-layouts  16 us
    all_gather x1, waiting for transfers between devices, local(): lax.all_gather(head_weight, 'src', axis=1, tiled=True)  15 us
  transfers between devices with their start and end apart: 5, of which 5 were waited for; matrix products, arithmetic and copies ran while one was open for 3% of the time, Pallas kernels for 0%

commit v1 on v0

v1 whole, which is shorter than its diff:
```python
import functools

import jax
import jax.numpy as jnp
import ml_dtypes
import numpy as np
from jax import lax
from jax.experimental import pallas as pl
from jax.experimental.pallas import tpu as pltpu
from jax.sharding import PartitionSpec as P

GRID = 16
SUB = 8
W = 32
PIX = 64
PATCH = 256
ORD = 128
HEADW = 768


def split_two(table):
    high = table.astype(ml_dtypes.bfloat16)
    low = (table - high.astype(np.float64)).astype(ml_dtypes.bfloat16)
    return high, low


def image_tables():
    angle = 2 * np.pi * (np.outer(np.arange(ORD), np.arange(PIX)) % PIX) / PIX
    c, s = np.cos(angle), np.sin(angle)
    one = np.block([[c, s, -s, c], [-s, c, -c, -s]])
    table_one = np.concatenate(split_two(one), 1)
    angle = 2 * np.pi * (np.outer(np.arange(PIX), np.arange(W)) % PIX) / PIX
    high, low = split_two(np.concatenate([np.cos(angle), np.sin(angle)], 1))
    table_two = np.concatenate([high, low, high], 1)
    spread = np.zeros((2 * SUB, SUB, 2 * SUB, GRID, SUB), ml_dtypes.bfloat16)
    for cu in range(2 * SUB):
        for v in range(SUB):
            spread[cu, v, cu, :, v] = 1
    spread = spread.reshape(2 * SUB * SUB, 2 * SUB * ORD)
    gather = np.repeat(np.eye(GRID), GRID, 1).astype(ml_dtypes.bfloat16)
    return spread, gather, table_one, table_two


def image_kernel(
    sources, index_ref, cutoff_ref, weight_ref, coeffs_ref, spread_ref, gather_ref,
    one_ref, two_ref, out_ref, spectra,
):
    row = lax.broadcasted_iota(jnp.int32, (PATCH, 2 * SUB * ORD), 0)
    lane = lax.broadcasted_iota(jnp.int32, (PATCH, 2 * SUB * ORD), 1)
    own = (row % GRID) == ((lane % ORD) // SUB)
    for pair in range(6):
        wide = jnp.dot(
            coeffs_ref[:, pair * 128:(pair + 1) * 128], spread_ref[...],
            preferred_element_type=jnp.float32,
        )
        kept = jnp.where(own, wide, 0.0).astype(jnp.bfloat16)
        rows = jnp.dot(gather_ref[...], kept, preferred_element_type=jnp.float32)
        for part in range(2):
            for u in range(SUB):
                at = (part * SUB + u) * ORD
                spectra[2 * pair + part, pl.ds(u, GRID, stride=SUB), :] = rows[:, at:at + ORD]

    order_i = lax.broadcasted_iota(jnp.int32, (W, ORD), 0) - W // 2
    order_j = lax.broadcasted_iota(jnp.int32, (W, ORD), 1) - W // 2

    def add_source(s, total):
        x0 = index_ref[2 * s]
        y0 = index_ref[2 * s + 1]
        radius = cutoff_ref[s]
        col = order_j - y0
        inside = (order_i * order_i + col * col <= radius * radius) & (col < W // 2)
        window = spectra[:, pl.ds(x0, W), :]
        window = jnp.where(inside[None], window, 0.0)
        both = jnp.concatenate(
            [jnp.concatenate([window[2 * k], window[2 * k + 1]], 1) for k in range(6)], 0
        ).astype(jnp.bfloat16)
        half = jnp.dot(both, one_ref[...], preferred_element_type=jnp.float32)
        half = half[:, :256] + half[:, 256:]
        high = half.astype(jnp.bfloat16)
        low = (half - high.astype(jnp.float32)).astype(jnp.bfloat16)

        def stacked(part):
            return jnp.concatenate(
                [
                    jnp.concatenate(
                        [part[k * W:(k + 1) * W, :128], part[k * W:(k + 1) * W, 128:]], 0
                    )
                    for k in range(6)
                ],
                1,
            )

        high, low = stacked(high), stacked(low)
        field = jnp.dot(
            two_ref[...], jnp.concatenate([high, high, low], 0),
            preferred_element_type=jnp.float32,
        )
        field = field * field
        power = field[:, :128]
        for k in range(1, 6):
            power = power + field[:, k * 128:(k + 1) * 128]
        return total + weight_ref[s] * power

    total = lax.fori_loop(0, sources, add_source, jnp.zeros((PIX, 128), jnp.float32), unroll=4)
    out_ref[...] = (total[:, :PIX] + total[:, PIX:]) * (1.0 / (6.0 * W * W * sources))


def image(coeffs, source_index, source_cutoff, source_weight):
    sources = source_weight.shape[0]
    smem = pl.BlockSpec(memory_space=pltpu.SMEM)
    vmem = pl.BlockSpec(memory_space=pltpu.VMEM)
    tables = [jnp.asarray(t) for t in image_tables()]
    out = pl.pallas_call(
        functools.partial(image_kernel, sources),
        out_shape=jax.ShapeDtypeStruct((PIX, PIX), jnp.float32),
        in_specs=[smem] * 3 + [vmem] * 5,
        out_specs=vmem,
        scratch_shapes=[pltpu.VMEM((12, ORD, ORD), jnp.float32)],
        compiler_params=pltpu.CompilerParams(vmem_limit_bytes=48 * 1024 * 1024),
        name="image_kernel",
    )(source_index.reshape(-1), source_cutoff, source_weight, coeffs, *tables)
    return out.reshape(1, PIX * PIX)


def local(
    tile_tokens, norm_gain, up_weight, down_weight, head_weight,
    source_index, source_cutoff, source_weight,
):
    groups = lax.axis_size("src")
    mine = lax.axis_index("src")
    ff = up_weight.shape[1]
    quarter = ff // groups
    folded = jnp.dot(
        down_weight, head_weight, preferred_element_type=jnp.float32
    ).astype(jnp.bfloat16)
    folded = lax.all_gather(folded, "src", axis=1, tiled=True)
    folded = lax.all_gather(folded, "tile", axis=0, tiled=True)
    folded = lax.dynamic_slice_in_dim(folded, mine * quarter, quarter, 0)
    up = lax.dynamic_slice_in_dim(up_weight, mine * quarter, quarter, 1)
    up = lax.all_gather(up, "tile", axis=0, tiled=True)
    tokens = lax.all_gather(tile_tokens, "src", axis=0, tiled=True)
    residual = tokens.astype(jnp.float32)
    mean_square = jnp.mean(residual * residual, axis=1, keepdims=True)
    normed = (residual * lax.rsqrt(mean_square + 1e-05) * norm_gain).astype(jnp.bfloat16)
    hidden = jax.nn.gelu(
        jnp.dot(normed, up, preferred_element_type=jnp.float32)
    ).astype(jnp.bfloat16)
    part = jnp.dot(hidden, folded, preferred_element_type=jnp.float32)
    kept = jnp.dot(tokens, head_weight, preferred_element_type=jnp.float32)
    part = lax.dynamic_update_slice_in_dim(
        part,
        lax.dynamic_slice_in_dim(part, mine * kept.shape[1], kept.shape[1], 1) + kept,
        mine * kept.shape[1], 1,
    )
    coeffs = lax.psum_scatter(part, "src", scatter_dimension=0, tiled=True).astype(jnp.bfloat16)
    return image(coeffs, source_index, source_cutoff, source_weight)


def solution(mesh):
    return jax.shard_map(
        local,
        mesh=mesh,
        in_specs=(
            P(("tile", "src"), None), P(), P("tile", None), P("tile", None),
            P(None, "src"), P(), P(), P(),
        ),
        out_specs=P(("tile", "src"), None),
        check_vma=False,
    )
```

time: 597 us -> 262 us (0.44)
  waiting for transfers between devices: 436 us -> 196 us
  local copies, waits for them, and re-layouts: 60.1 us -> 10 us
  matrix products: 41.7 us -> 16.5 us
  loops' own time: 21.2 us -> 0 us
  Pallas kernels: 0 us -> 12.3 us
  other arithmetic: 14.9 us -> 4.25 us
  blocking collectives: 0 us -> 8.87 us
    all_gather x3, waiting for transfers between devices: 345 us -> 159 us  [the longest x1 75.5 us: local(): folded = lax.all_gather(folded, 'tile', axis=0, tiled=True)]
    psum x1 -> x0, waiting for transfers between devices: 66.8 us -> none  [local(): everything = lax.psum(image_sum, 'tile')]
    reduce_scatter x0 -> x1, waiting for transfers between devices: none -> 36.7 us  [local(): lax.psum_scatter(part, 'src', scatter_dimension=0, tiled=True)]
    dot_general x10 -> x3, matrix products: 41.7 us -> 16.5 us  [the longest x1 10.3 us: local(): part = jnp.dot(hidden, folded, preferred_element_type=jnp.float32)]
    all_to_all x1 -> x0, waiting for transfers between devices: 22.9 us -> none  [local(): lax.all_to_all(cut_blocks, 'tile', split_axis=0, concat_axis=1, tiled=True)]
    another operation x2 -> x0, loops' own time: 21.2 us -> none  [the longest x1 21 us: local(): lax.scan(add_source, running, (local_index, local_cutoff, local_weight))]
    gather x24 -> x0, local copies, waits for them, and re-layouts: 16 us -> none
    reshape x9 -> x2, local copies, waits for them, and re-layouts: 16.7 us -> 0.8 us  [the longest x1 0.69 us: image(): return out.reshape(1, PIX * PIX)]
  transfers between devices with their start and end apart: 5 -> 4, of which waited for: 5 -> 4; matrix products, arithmetic and copies ran while one was open for 3% -> 3% of each run, Pallas kernels for 0% -> 0%
where the time goes in v1:
time: 262 us; the launch traced here: 261 us
  waiting for transfers between devices  196 us (75%)
  matrix products  16.5 us (6%)
  between operations  13.3 us (5%)
  Pallas kernels  12.3 us (5%)
  local copies, waits for them, and re-layouts  10 us (4%)
  blocking collectives  8.87 us (3%)
  other arithmetic  4.25 us (2%)
    all_gather x1, waiting for transfers between devices, local(): folded = lax.all_gather(folded, 'tile', axis=0, tiled=True)  75.5 us
    all_gather x1, waiting for transfers between devices, local(): up = lax.all_gather(up, 'tile', axis=0, tiled=True)  58.3 us
    reduce_scatter x1, waiting for transfers between devices, local(): lax.psum_scatter(part, 'src', scatter_dimension=0, tiled=True)  36.7 us
    all_gather x1, waiting for transfers between devices, local(): tokens = lax.all_gather(tile_tokens, 'src', axis=0, tiled=True)  24.8 us
    pallas_call x1, Pallas kernels, image(): pl.pallas_call(functools.partial(image_kernel, sources), out_shape=jax.Sh...  12.3 us
    dot_general x1, matrix products, local(): part = jnp.dot(hidden, folded, preferred_element_type=jnp.float32)  10.3 us
    all_gather x1, blocking collectives, local(): folded = lax.all_gather(folded, 'src', axis=1, tiled=True)  8.87 us
    dynamic_update_slice x1, local copies, waits for them, and re-layouts, local(): lax.dynamic_update_slice_in_dim(part, lax.dynamic_slice_in_dim(part, mine...  6.51 us
  transfers between devices with their start and end apart: 4, of which 4 were waited for; matrix products, arithmetic and copies ran while one was open for 3% of the time, Pallas kernels for 0%

profile of v1, /device:TPU:1, one launch (start us, length us, event | category | flops | bytes accessed | tf_op | source)
XLA Modules:
  0.0 261.4 jit_solution(12946104496923804083)
XLA Ops:
  6.5 0.7 all-gather.4.cloned.1.call-update
  7.3 0.0 all-gather.6.cloned.1.call-start
  7.3 0.6 copy-done
  7.9 0.9 constant_dynamic-slice_fusion
  8.8 0.0 all-gather.6.cloned.1.call-update
  8.9 0.0 all-gather.8.cloned.1.call-start
  8.9 2.2 convolution_convert_fusion
  11.2 8.9 %all_gather.14 = bf16[352,768]{0,1:T(8,128)(2,1)S(1)} all-gather(bf16[352,192]{0,1:T(8,128)(2,1)S(1)} %convolution_convert_fusion), channel_id=1, replica_groups=mesh['tile'=8,'src'=4] {'src'}, dimensions={1}, use_global_device_ids=true | all-gather | bytes 675840 | tf_op jit(solution)/shard_map/all_gather | solution.py:136
  20.0 1.0 copy.26
  21.1 0.0 reduce-scatter.2.cloned.1.call-start
  21.2 24.8 %all-gather.4.cloned.1.call-done = bf16[1024,2048]{1,0:T(8,128)(2,1)} async-done(((bf16[256,2048]{1,0:T(8,128)(2,1)}), bf16[1024,2048]{1,0:T(8,128)(2,1)}) %all-gather.4.cloned.1.call-update) | async-done | bytes 4194320 | tf_op jit(solution)/shard_map/all_gather | solution.py:141
  45.9 3.1 %fusion = f32[1024]{0:T(1024)S(1)} fusion(bf16[1024,2048]{1,0:T(8,128)(2,1)} %all-gather.4.cloned.1.call-done), kind=kLoop, calls=%fused_computation.2 | loop fusion | flops 6290432 | bytes 4198400 | tf_op jit(solution)/shard_map/reduce_sum | solution.py:143
  49.0 58.3 %all-gather.6.cloned.1.call-done = bf16[2048,704]{1,0:T(8,128)(2,1)} async-done(((bf16[256,704]{1,0:T(8,128)(2,1)}), bf16[2048,704]{1,0:T(8,128)(2,1)}) %all-gather.6.cloned.1.call-update) | async-done | bytes 2883600 | tf_op jit(solution)/shard_map/all_gather | solution.py:140
  107.4 75.5 %all-gather.8.cloned.1.call-done = bf16[2816,768]{1,0:T(8,128)(2,1)} async-done(((bf16[352,768]{1,0:T(8,128)(2,1)}), bf16[2816,768]{1,0:T(8,128)(2,1)}) %all-gather.8.cloned.1.call-update) | async-done | bytes 4325392 | tf_op jit(solution)/shard_map/all_gather | solution.py:137
  182.8 10.3 %fusion.17 = f32[1024,768]{1,0:T(8,128)} fusion(bf16[2816,768]{1,0:T(8,128)(2,1)} %all-gather.8.cloned.1.call-done, s32[]{:T(128)S(6)} %select_n.8, bf16[2048,704]{1,0:T(8,128)(2,1)} %all-gather.6.cloned.1.call-done, bf16[1024,2048]{1,0:T(8,128)(2,1)} %all-gather.4.cloned.1.call-done, f32[2048]{0:T(1024)S(1)} %copy-done.9, f32[1024]{0:T(1024)S(1)} %add_rsqrt_fusion), kind=kOutput, calls=%fused_computation.19 | convolution fusion | flops 4074962944 | bytes 11579396 | tf_op jit(solution)/shard_map/dot_general | solution.py:148
  193.1 3.9 %convolution_add_fusion = f32[1024,192]{1,0:T(8,128)S(1)} fusion(bf16[1024,2048]{1,0:T(8,128)(2,1)} %all-gather.4.cloned.1.call-done, bf16[2048,192]{0,1:T(8,128)(2,1)S(1)} %copy-done.8, f32[1024,768]{1,0:T(8,128)} %fusion.17, s32[]{:T(128)S(6)} %select_n.9), kind=kOutput, calls=%fused_computation.17 | convolution fusion | flops 805502976 | bytes 6553604 | tf_op jit(solution)/shard_map/dot_general | solution.py:149
  197.1 6.5 %dynamic_update_slice.3 = f32[1024,768]{1,0:T(8,128)} dynamic-update-slice(f32[1024,768]{1,0:T(8,128)} %fusion.17, f32[1024,192]{1,0:T(8,128)S(1)} %convolution_add_fusion, s32[]{:T(128)} %constant.8.clone.1, s32[]{:T(128)S(6)} %select_n.9) | dynamic-update-slice | bytes 1572868 | tf_op jit(solution)/shard_map/dynamic_update_slice | solution.py:150
  203.7 0.0 reduce-scatter.2.cloned.1.call-update
  203.7 0.1 copy.25
  203.8 0.1 reshape.15.index_ref
  203.9 36.7 %reduce-scatter.2.cloned.1.call-done = f32[256,768]{1,0:T(8,128)} async-done(((f32[1024,768]{1,0:T(8,128)}), f32[256,768]{1,0:T(8,128)}) %reduce-scatter.2.cloned.1.call-update) | async-done | bytes 786448 | tf_op jit(solution)/shard_map/reduce_scatter | solution.py:155
  240.6 1.2 convert_element_type.19.coeffs_ref
  241.8 12.3 %image_kernel.1 = f32[64,64]{1,0:T(8,128)S(1)} custom-call(s32[64]{0:T(128)S(1)} %reshape.15.index_ref, s32[32]{0:T(128)S(1)} %copy-done.5, f32[32]{0:T(128)S(1)} %copy-done.6, bf16[256,768]{1,0:T(8,128)(2,1)S(1)} %convert_element_type.19.coeffs_ref, bf16[128,2048]{1,0:T(8,128)(2,1)S(1)} %copy-done.1, bf16[16,256]{1,0:T(8,128)(2,1)S(1)} %copy-done.4, ...), custom_call_target="tpu_custom_call" | custom-call | tf_op jit(solution)/shard_map/image_kernel/pallas_call | solution.py:113
  254.2 0.7 reshape.16
  (22 shorter events, 0.1 us)
Async XLA Ops:
  6.5 1.4 copy-start
  6.5 39.4 %all-gather.4.cloned.1.call-start = ((), (), s32[]{:S(2)}) async-start(), calls=%async_computation.1 | async-start | bytes 5242880 | tf_op jit(solution)/shard_map/all_gather | solution.py:141
  7.3 100.1 %all-gather.6.cloned.1.call-start = ((), (), s32[]{:S(2)}) async-start(), calls=%async_computation.2 | async-start | bytes 3538944 | tf_op jit(solution)/shard_map/all_gather | solution.py:140
  8.9 174.0 %all-gather.8.cloned.1.call-start = ((), (), s32[]{:S(2)}) async-start(), calls=%async_computation.3 | async-start | bytes 4866048 | tf_op jit(solution)/shard_map/all_gather | solution.py:137
  11.2 171.7 %copy-start.9 = (f32[2048]{0:T(1024)S(1)}, f32[2048]{0:T(1024)}, u32[]{:S(2)}) copy-start(f32[2048]{0:T(1024)} %param.13) | copy-start | bytes 24580
  21.1 219.5 %reduce-scatter.2.cloned.1.call-start = ((), (), s32[]{:S(2)}) async-start(), calls=%async_computation.4 | async-start | bytes 3932160 | tf_op jit(solution)/shard_map/reduce_scatter | solution.py:155
  49.0 144.1 %copy-start.8 = (bf16[2048,192]{0,1:T(8,128)(2,1)S(1)}, bf16[2048,192]{0,1:T(8,128)(2,1)}, u32[]{:S(2)}) copy-start(bf16[2048,192]{0,1:T(8,128)(2,1)} %param.16) | copy-start | bytes 2359300
  197.1 6.6 %copy-start.7 = (s32[32,2]{0,1:T(2,128)S(1)}, s32[32,2]{0,1:T(2,128)}, u32[]{:S(2)}) copy-start(s32[32,2]{0,1:T(2,128)} %param.17) | copy-start | bytes 772
  197.1 44.7 %copy-start.1 = (bf16[128,2048]{1,0:T(8,128)(2,1)S(1)}, bf16[128,2048]{1,0:T(8,128)(2,1)}, u32[]{:S(2)}) copy-start(bf16[128,2048]{1,0:T(8,128)(2,1)} %constant.37.clone.spread_ref) | copy-start | bytes 1572868
  197.1 44.7 %copy-start.2 = (bf16[256,512]{1,0:T(8,128)(2,1)S(1)}, bf16[256,512]{1,0:T(8,128)(2,1)}, u32[]{:S(2)}) copy-start(bf16[256,512]{1,0:T(8,128)(2,1)} %constant.39.clone.one_ref) | copy-start | bytes 786436
  197.1 44.7 %copy-start.3 = (bf16[64,192]{1,0:T(8,128)(2,1)S(1)}, bf16[64,192]{1,0:T(8,128)(2,1)}, u32[]{:S(2)}) copy-start(bf16[64,192]{1,0:T(8,128)(2,1)} %constant.40.clone.two_ref) | copy-start | bytes 73732
  197.1 44.7 %copy-start.4 = (bf16[16,256]{1,0:T(8,128)(2,1)S(1)}, bf16[16,256]{1,0:T(8,128)(2,1)}, u32[]{:S(2)}) copy-start(bf16[16,256]{1,0:T(8,128)(2,1)} %constant.38.clone.gather_ref) | copy-start | bytes 24580
  197.1 44.7 %copy-start.5 = (s32[32]{0:T(128)S(1)}, s32[32]{0:T(128)}, u32[]{:S(2)}) copy-start(s32[32]{0:T(128)} %cutoff_ref.1) | copy-start | bytes 388
  197.1 44.7 %copy-start.6 = (f32[32]{0:T(128)S(1)}, f32[32]{0:T(128)}, u32[]{:S(2)}) copy-start(f32[32]{0:T(128)} %weight_ref.1) | copy-start | bytes 388
Sparse Core Ops, SparseCore 0:
  8.9 36.9 all-gather.3
  48.1 59.1 all-gather.5
  109.5 73.2 all-gather.7
  203.8 36.7 reduce-scatter.1

commit v2 on v1

--- a/solution.py
+++ b/solution.py
@@ -122,6 +122,271 @@
     return out.reshape(1, PIX * PIX)
 
 
+MESH = pl.DeviceIdType.MESH
+
+
+def surrogate_kernel(
+    tiles, groups, tok_ref, gain_ref, up_ref, down_ref, head_ref, out_ref,
+    tok_buf, norm_buf, up_buf, acc, block, block_in, fold_own, fold_buf, fold_all,
+    part, mine_part, sib_buf, cross_out, cross_in,
+    up_send, up_fsend, up_recv, tok_send, tok_fsend, tok_recv, block_send, block_recv,
+    fold_send, fold_fsend, fold_recv, sib_send, sib_recv, cross_send, cross_recv,
+):
+    t, s = lax.axis_index("tile"), lax.axis_index("src")
+    tile_pairs, chips = tiles // 2, groups // 2
+    side, pair = lax.rem(t, 2), t // 2
+    core, chip = lax.rem(s, 2), s // 2
+    width = head_ref.shape[1]
+    depth = up_ref.shape[0]
+    share = tiles // groups
+    owner = t // share
+
+    def send(source, target, sent, got, tile, col):
+        return pltpu.make_async_remote_copy(
+            src_ref=source, dst_ref=target, send_sem=sent, recv_sem=got,
+            device_id={"tile": tile, "src": col}, device_id_type=MESH,
+        )
+
+    def tile_at(k):
+        return 2 * lax.rem(pair + k, tile_pairs) + side
+
+    def col_at(k):
+        return 2 * lax.rem(chip + k, chips) + core
+
+    tile_mate = t + 1 - 2 * side
+    col_mate = s + 1 - 2 * core
+
+    barrier = pltpu.get_barrier_semaphore()
+    for k in range(1, tile_pairs):
+        pl.semaphore_signal(barrier, inc=1, device_id={"tile": tile_at(k), "src": s}, device_id_type=MESH)
+    pl.semaphore_signal(barrier, inc=1, device_id={"tile": tile_mate, "src": s}, device_id_type=MESH)
+    for k in range(1, groups):
+        pl.semaphore_signal(
+            barrier, inc=1, device_id={"tile": t, "src": lax.rem(s + k, groups)}, device_id_type=MESH
+        )
+    pl.semaphore_wait(barrier, tile_pairs + groups - 1)
+
+    up_copies = [
+        send(up_ref, up_buf.at[t], up_send.at[k], up_recv.at[t], tile_mate if k == 0 else tile_at(k), s)
+        for k in range(tile_pairs)
+    ]
+    tok_copies = [
+        send(tok_ref, tok_buf.at[s], tok_send.at[k], tok_recv.at[s], t, col_mate if k == 0 else col_at(k))
+        for k in range(chips)
+    ]
+    for copy in tok_copies[1:] + up_copies[1:] + tok_copies[:1] + up_copies[:1]:
+        copy.start()
+
+    block[...] = jnp.dot(
+        down_ref[...], head_ref[...], preferred_element_type=jnp.float32
+    ).astype(jnp.bfloat16)
+    block_copy = send(block, block_in.at[s], block_send, block_recv.at[s], t, owner)
+
+    @pl.when(s != owner)
+    def _():
+        block_copy.start()
+
+    def normalise(source, col):
+        value = source[...].astype(jnp.float32)
+        square = jnp.mean(value * value, axis=1, keepdims=True)
+        value = (value * lax.rsqrt(square + 1e-05) * gain_ref[...]).astype(jnp.bfloat16)
+        for j in range(tiles):
+            norm_buf[j, col] = value[:, j * depth:(j + 1) * depth]
+
+    normalise(tok_ref, s)
+
+    def fold_copy(k):
+        return send(
+            fold_own, fold_buf.at[lax.rem(t, share)], fold_send.at[k],
+            fold_recv.at[lax.rem(t, share)], tile_mate if k == 0 else tile_at(k), s,
+        )
+
+    @pl.when(s == owner)
+    def _():
+        for k in range(1, groups):
+            col = lax.rem(s + k, groups)
+            send(block, block_in.at[col], block_send, block_recv.at[col], t, s).wait_recv()
+        for q in range(groups):
+            @pl.when(s == q)
+            def _():
+                fold_own[:, q * width:(q + 1) * width] = block[...]
+
+            @pl.when(s != q)
+            def _():
+                fold_own[:, q * width:(q + 1) * width] = block_in[q]
+
+        for k in range(tile_pairs):
+            fold_copy(k).start()
+        fold_buf[lax.rem(t, share)] = fold_own[...]
+
+    def up_forward(k):
+        at = tile_at(k)
+        return send(up_buf.at[at], up_buf.at[at], up_fsend.at[k], up_recv.at[at], tile_mate, s)
+
+    def fold_forward(j):
+        at = 2 * j + side
+        return send(fold_buf.at[at], fold_buf.at[at], fold_fsend.at[j], fold_recv.at[at], tile_mate, s)
+
+    def fold_is_mine(j):
+        return pair == s * (share // 2) + j
+
+    def tok_forward(k):
+        at = col_at(k)
+        return send(tok_buf.at[at], tok_buf.at[at], tok_fsend.at[k], tok_recv.at[at], t, col_mate)
+
+    for k in range(1, tile_pairs):
+        up_forward(k).wait_recv()
+        up_forward(k).start()
+        if k == 1:
+            send(
+                tok_ref, tok_buf.at[col_mate], tok_send.at[0], tok_recv.at[col_mate], t, col_mate
+            ).wait_recv()
+            normalise(tok_buf.at[col_mate], col_mate)
+    for j in range(share // 2):
+        @pl.when(jnp.logical_not(fold_is_mine(j)))
+        def _():
+            fold_forward(j).wait_recv()
+            fold_forward(j).start()
+    for k in range(1, chips):
+        tok_forward(k).wait_recv()
+        tok_forward(k).start()
+    for k in range(1, chips):
+        normalise(tok_buf.at[col_at(k)], col_at(k))
+    for k in range(1, chips):
+        at = 2 * lax.rem(chip + k, chips) + 1 - core
+        send(tok_ref, tok_buf.at[at], tok_send.at[0], tok_recv.at[at], t, col_mate).wait_recv()
+        normalise(tok_buf.at[at], at)
+
+    def add_block(rows_ref, at, first=False):
+        def step(g, carry):
+            value = jnp.dot(norm_buf[at, g], rows_ref[...], preferred_element_type=jnp.float32)
+            if first:
+                acc[g] = value
+            else:
+                acc[g] = acc[g] + value
+            return carry
+        lax.fori_loop(0, groups, step, 0)
+
+    add_block(up_ref, t, True)
+    for k in range(1, tile_pairs):
+        add_block(up_buf.at[tile_at(k)], tile_at(k))
+    for k in range(tile_pairs):
+        at = 2 * lax.rem(pair + k, tile_pairs) + 1 - side
+        send(up_ref, up_buf.at[at], up_send.at[0], up_recv.at[at], tile_mate, s).wait_recv()
+        add_block(up_buf.at[at], at)
+    for j in range(share // 2):
+        at = 2 * j + 1 - side
+        send(fold_own, fold_buf.at[at], fold_send.at[0], fold_recv.at[at], tile_mate, s).wait_recv()
+    folded = jnp.concatenate([fold_buf[j].astype(jnp.float32) for j in range(share)], 0)
+    real = folded.shape[0]
+    fold_all[...] = jnp.zeros_like(fold_all)
+    fold_all[:real, :] = folded.astype(jnp.bfloat16)
+
+    def partial(col, target):
+        value = acc[col]
+        inner = 0.7978845608028654 * (value + 0.044715 * (value * value * value))
+        hidden = (0.5 * value * (1.0 + jnp.tanh(inner))).astype(jnp.bfloat16)
+        target[...] = jnp.dot(hidden, fold_all[...], preferred_element_type=jnp.float32)
+
+        def keep(source):
+            kept = jnp.dot(source[...], head_ref[...], preferred_element_type=jnp.float32)
+            for q in range(groups):
+                @pl.when(s == q)
+                def _():
+                    target[:, q * width:(q + 1) * width] += kept
+
+        keep(tok_buf.at[col])
+
+    tok_buf[s] = tok_ref[...]
+
+    def sib_copy(k):
+        return send(part.at[k], sib_buf.at[k], sib_send.at[k], sib_recv.at[k], t, col_mate)
+
+    def cross_copy(k):
+        return send(cross_out.at[k], cross_in.at[k], cross_send.at[k], cross_recv.at[k], t, col_at(k))
+
+    for k in list(range(1, chips)) + [0]:
+        partial(2 * lax.rem(chip + k, chips) + 1 - core, part.at[k])
+        sib_copy(k).start()
+        partial(col_at(k), mine_part)
+        sib_copy(k).wait_recv()
+        mine_part[...] += sib_buf[k]
+        if k > 0:
+            cross_out[k] = mine_part[...].astype(jnp.bfloat16)
+            cross_copy(k).start()
+    total = mine_part[...]
+    for k in range(1, chips):
+        cross_copy(k).wait_recv()
+        total = total + cross_in[k].astype(jnp.float32)
+    out_ref[...] = total.astype(jnp.bfloat16)
+
+    for copy in up_copies + tok_copies:
+        copy.wait_send()
+    for k in range(1, tile_pairs):
+        up_forward(k).wait_send()
+    for k in range(1, chips):
+        tok_forward(k).wait_send()
+        cross_copy(k).wait_send()
+    for k in range(chips):
+        sib_copy(k).wait_send()
+
+    @pl.when(s != owner)
+    def _():
+        block_copy.wait_send()
+
+    @pl.when(s == owner)
+    def _():
+        for k in range(tile_pairs):
+            fold_copy(k).wait_send()
+
+    for j in range(share // 2):
+        @pl.when(jnp.logical_not(fold_is_mine(j)))
+        def _():
+            fold_forward(j).wait_send()
+
+
+def surrogate(tokens, gain, up, down, head, tiles, groups):
+    rows, model = tokens.shape
+    depth, wide = up.shape
+    ff_rows, width = down.shape[0], head.shape[1]
+    outs = groups * width
+    share, chips = tiles // groups, groups // 2
+    dma = pltpu.SemaphoreType.DMA
+    bf16, f32 = jnp.bfloat16, jnp.float32
+    vmem = pl.BlockSpec(memory_space=pltpu.VMEM)
+    return pl.pallas_call(
+        functools.partial(surrogate_kernel, tiles, groups),
+        out_shape=jax.ShapeDtypeStruct((rows, outs), bf16),
+        in_specs=[vmem] * 5,
+        out_specs=vmem,
+        scratch_shapes=[
+            pltpu.VMEM((groups, rows, model), bf16),
+            pltpu.VMEM((tiles, groups, rows, depth), bf16),
+            pltpu.VMEM((tiles, depth, wide), bf16),
+            pltpu.VMEM((groups, rows, wide), f32),
+            pltpu.VMEM((ff_rows, width), bf16),
+            pltpu.VMEM((groups, ff_rows, width), bf16),
+            pltpu.VMEM((ff_rows, outs), bf16),
+            pltpu.VMEM((share, ff_rows, outs), bf16),
+            pltpu.VMEM((wide, outs), bf16),
+            pltpu.VMEM((chips, rows, outs), f32),
+            pltpu.VMEM((rows, outs), f32),
+            pltpu.VMEM((chips, rows, outs), f32),
+            pltpu.VMEM((chips, rows, outs), bf16),
+            pltpu.VMEM((chips, rows, outs), bf16),
+            dma((tiles // 2,)), dma((tiles // 2,)), dma((tiles,)),
+            dma((chips,)), dma((chips,)), dma((groups,)),
+            dma(()), dma((groups,)),
+            dma((tiles // 2,)), dma((share // 2,)), dma((share,)),
+            dma((chips,)), dma((chips,)), dma((chips,)), dma((chips,)),
+        ],
+        compiler_params=pltpu.CompilerParams(
+            collective_id=0, has_side_effects=True, vmem_limit_bytes=52 * 1024 * 1024
+        ),
+        name="surrogate_kernel",
+    )(tokens, gain.reshape(1, -1), up, down, head)
+
+
 def local(
     tile_tokens, norm_gain, up_weight, down_weight, head_weight,
     source_index, source_cutoff, source_weight,
@@ -130,29 +395,12 @@
     mine = lax.axis_index("src")
     ff = up_weight.shape[1]
     quarter = ff // groups
-    folded = jnp.dot(
-        down_weight, head_weight, preferred_element_type=jnp.float32
-    ).astype(jnp.bfloat16)
-    folded = lax.all_gather(folded, "src", axis=1, tiled=True)
-    folded = lax.all_gather(folded, "tile", axis=0, tiled=True)
-    folded = lax.dynamic_slice_in_dim(folded, mine * quarter, quarter, 0)
+    wide = -(-quarter // 256) * 256
     up = lax.dynamic_slice_in_dim(up_weight, mine * quarter, quarter, 1)
-    up = lax.all_gather(up, "tile", axis=0, tiled=True)
-    tokens = lax.all_gather(tile_tokens, "src", axis=0, tiled=True)
-    residual = tokens.astype(jnp.float32)
-    mean_square = jnp.mean(residual * residual, axis=1, keepdims=True)
-    normed = (residual * lax.rsqrt(mean_square + 1e-05) * norm_gain).astype(jnp.bfloat16)
-    hidden = jax.nn.gelu(
-        jnp.dot(normed, up, preferred_element_type=jnp.float32)
-    ).astype(jnp.bfloat16)
-    part = jnp.dot(hidden, folded, preferred_element_type=jnp.float32)
-    kept = jnp.dot(tokens, head_weight, preferred_element_type=jnp.float32)
-    part = lax.dynamic_update_slice_in_dim(
-        part,
-        lax.dynamic_slice_in_dim(part, mine * kept.shape[1], kept.shape[1], 1) + kept,
-        mine * kept.shape[1], 1,
+    up = jnp.pad(up, ((0, 0), (0, wide - quarter)))
+    coeffs = surrogate(
+        tile_tokens, norm_gain, up, down_weight, head_weight, lax.axis_size("tile"), groups
     )
-    coeffs = lax.psum_scatter(part, "src", scatter_dimension=0, tiled=True).astype(jnp.bfloat16)
     return image(coeffs, source_index, source_cutoff, source_weight)
 
 

time: 262 us -> 125 us (0.48)
  the two profiles are of different devices: /device:TPU:1 before, /device:TPU:9 now
where the time goes in v2:
time: 125 us
  Pallas kernels  116 us (93%)
  local copies, waits for them, and re-layouts  8.58 us (7%)
    pallas_call x1, Pallas kernels, surrogate(): pl.pallas_call(functools.partial(surrogate_kernel, tiles, groups), out_sh...  104 us
    pallas_call x1, Pallas kernels, image(): pl.pallas_call(functools.partial(image_kernel, sources), out_shape=jax.Sh...  12.3 us
    unnamed x20, local copies, waits for them, and re-layouts  7.55 us

profile of v2, /device:TPU:9, one launch (start us, length us, event | category | flops | bytes accessed | tf_op | source)
XLA Modules:
  0.0 124.6 jit_solution(14191851828548067513)
XLA Ops:
  0.0 0.0 copy-start
  0.0 1.4 %copy-done = bf16[256,2816]{1,0:T(8,128)(2,1)S(1)} copy-done((bf16[256,2816]{1,0:T(8,128)(2,1)S(1)}, bf16[256,2816]{1,0:T(8,128)(2,1)}, u32[]{:S(2)}) %copy-start) | copy-done | bytes 1441816
  1.4 0.2 constant_dynamic-slice_fusion
  1.6 0.0 copy-start.1
  1.6 0.0 copy-start.5
  1.6 2.3 %copy.16.head_ref = bf16[2048,192]{1,0:T(8,128)(2,1)} copy(bf16[2048,192]{0,1:T(8,128)(2,1)} %param.16) | data formatting | bytes 1572864 | tf_op args[4]
  3.9 0.0 copy-done.1
  3.9 0.0 copy-done.5
  3.9 0.0 copy-start.3
  3.9 0.0 copy-start.6
  4.0 103.6 %surrogate_kernel.1.coeffs_ref = bf16[256,768]{1,0:T(8,128)(2,1)S(1)} custom-call(bf16[256,2048]{1,0:T(8,128)(2,1)S(1)} %copy-done.1, f32[1,2048]{1,0:T(1,128)S(1)} %bitcast.1, bf16[256,768]{1,0:T(8,128)(2,1)S(1)} %pad.4.up_ref, bf16[352,2048]{1,0:T(8,128)(2,1)} %down_ref.1, bf16[2048,192]{1,0:T(8,128)(2,1)} %copy.16.head_ref), custom_call_target="tpu_custom_call" | custom-call | tf_op jit(solution)/shard_map/surrogate_kernel/pallas_call | solution.py:357
  107.6 0.8 copy.15
  108.4 0.1 reshape.9.index_ref
  108.5 0.0 copy-done.3
  108.5 0.0 copy-done.6
  108.5 0.0 copy-start.2
  108.5 1.0 copy-done.2
  109.5 0.0 copy-start.4
  109.5 0.8 copy-done.4
  110.3 0.0 copy-start.7
  110.3 0.7 copy-done.7
  111.0 0.7 copy-done.8
  111.6 12.3 %image_kernel.1 = f32[64,64]{1,0:T(8,128)S(1)} custom-call(s32[64]{0:T(128)S(1)} %reshape.9.index_ref, s32[32]{0:T(128)S(1)} %copy-done.7, f32[32]{0:T(128)S(1)} %copy-done.8, bf16[256,768]{1,0:T(8,128)(2,1)S(1)} %surrogate_kernel.1.coeffs_ref, bf16[128,2048]{1,0:T(8,128)(2,1)S(1)} %copy-done.2, bf16[16,256]{1,0:T(8,128)(2,1)S(1)} %copy-done.6, ...), custom_call_target="tpu_custom_call" | custom-call | tf_op jit(solution)/shard_map/image_kernel/pallas_call | solution.py:113
  123.9 0.7 reshape.11
  (2 shorter events, 0.0 us)
Async XLA Ops:
  0.0 1.4 %copy-start = (bf16[256,2816]{1,0:T(8,128)(2,1)S(1)}, bf16[256,2816]{1,0:T(8,128)(2,1)}, u32[]{:S(2)}) copy-start(bf16[256,2816]{1,0:T(8,128)(2,1)} %param.14) | copy-start | bytes 4325380
  1.6 2.4 %copy-start.1 = (bf16[256,2048]{1,0:T(8,128)(2,1)S(1)}, bf16[256,2048]{1,0:T(8,128)(2,1)}, u32[]{:S(2)}) copy-start(bf16[256,2048]{1,0:T(8,128)(2,1)} %tok_ref.1) | copy-start | bytes 3145732
  1.6 2.4 %copy-start.5 = (f32[2048]{0:T(1024)S(1)}, f32[2048]{0:T(1024)}, u32[]{:S(2)}) copy-start(f32[2048]{0:T(1024)} %param.13) | copy-start | bytes 24580
  3.9 104.5 %copy-start.3 = (bf16[256,512]{1,0:T(8,128)(2,1)S(1)}, bf16[256,512]{1,0:T(8,128)(2,1)}, u32[]{:S(2)}) copy-start(bf16[256,512]{1,0:T(8,128)(2,1)} %constant.22.clone.one_ref) | copy-start | bytes 786436
  3.9 104.5 %copy-start.6 = (bf16[16,256]{1,0:T(8,128)(2,1)S(1)}, bf16[16,256]{1,0:T(8,128)(2,1)}, u32[]{:S(2)}) copy-start(bf16[16,256]{1,0:T(8,128)(2,1)} %constant.21.clone.gather_ref) | copy-start | bytes 24580
  108.5 1.0 copy-start.2
  109.5 0.8 copy-start.4
  110.3 0.7 copy-start.7
  111.0 0.7 copy-start.8

commit v3 on v2

--- a/solution.py
+++ b/solution.py
@@ -116,7 +116,7 @@
         in_specs=[smem] * 3 + [vmem] * 5,
         out_specs=vmem,
         scratch_shapes=[pltpu.VMEM((12, ORD, ORD), jnp.float32)],
-        compiler_params=pltpu.CompilerParams(vmem_limit_bytes=48 * 1024 * 1024),
+        compiler_params=pltpu.CompilerParams(vmem_limit_bytes=24 * 1024 * 1024),
         name="image_kernel",
     )(source_index.reshape(-1), source_cutoff, source_weight, coeffs, *tables)
     return out.reshape(1, PIX * PIX)
@@ -128,9 +128,9 @@
 def surrogate_kernel(
     tiles, groups, tok_ref, gain_ref, up_ref, down_ref, head_ref, out_ref,
     tok_buf, norm_buf, up_buf, acc, block, block_in, fold_own, fold_buf, fold_all,
-    part, mine_part, sib_buf, cross_out, cross_in,
-    up_send, up_fsend, up_recv, tok_send, tok_fsend, tok_recv, block_send, block_recv,
-    fold_send, fold_fsend, fold_recv, sib_send, sib_recv, cross_send, cross_recv,
+    part, mine_part, sib_buf, cross_out, cross_in, kept_buf,
+    up_send, up_fsend, up_lsend, up_recv, tok_send, tok_fsend, tok_recv, block_send, block_recv,
+    fold_send, fold_fsend, fold_lsend, fold_recv, sib_send, sib_recv, cross_send, cross_recv,
 ):
     t, s = lax.axis_index("tile"), lax.axis_index("src")
     tile_pairs, chips = tiles // 2, groups // 2
@@ -150,6 +150,9 @@
     def tile_at(k):
         return 2 * lax.rem(pair + k, tile_pairs) + side
 
+    def line(step):
+        return (pair + step >= 0) & (pair + step < tile_pairs)
+
     def col_at(k):
         return 2 * lax.rem(chip + k, chips) + core
 
@@ -157,24 +160,33 @@
     col_mate = s + 1 - 2 * core
 
     barrier = pltpu.get_barrier_semaphore()
-    for k in range(1, tile_pairs):
-        pl.semaphore_signal(barrier, inc=1, device_id={"tile": tile_at(k), "src": s}, device_id_type=MESH)
+    for step in (-1, 1):
+        @pl.when(line(step))
+        def _():
+            pl.semaphore_signal(
+                barrier, inc=1, device_id={"tile": t + 2 * step, "src": s}, device_id_type=MESH
+            )
     pl.semaphore_signal(barrier, inc=1, device_id={"tile": tile_mate, "src": s}, device_id_type=MESH)
     for k in range(1, groups):
         pl.semaphore_signal(
             barrier, inc=1, device_id={"tile": t, "src": lax.rem(s + k, groups)}, device_id_type=MESH
         )
-    pl.semaphore_wait(barrier, tile_pairs + groups - 1)
-
-    up_copies = [
-        send(up_ref, up_buf.at[t], up_send.at[k], up_recv.at[t], tile_mate if k == 0 else tile_at(k), s)
-        for k in range(tile_pairs)
-    ]
+    pl.semaphore_wait(barrier, groups + line(-1).astype(jnp.int32) + line(1).astype(jnp.int32))
+
+    up_mate = send(up_ref, up_buf.at[t], up_send.at[0], up_recv.at[t], tile_mate, s)
+    up_line = {
+        step: send(up_ref, up_buf.at[t], up_send.at[(3 + step) // 2], up_recv.at[t], t + 2 * step, s)
+        for step in (-1, 1)
+    }
     tok_copies = [
         send(tok_ref, tok_buf.at[s], tok_send.at[k], tok_recv.at[s], t, col_mate if k == 0 else col_at(k))
         for k in range(chips)
     ]
-    for copy in tok_copies[1:] + up_copies[1:] + tok_copies[:1] + up_copies[:1]:
+    for step in (-1, 1):
+        @pl.when(line(step))
+        def _():
+            up_line[step].start()
+    for copy in tok_copies[1:] + [up_mate] + tok_copies[:1]:
         copy.start()
 
     block[...] = jnp.dot(
@@ -193,13 +205,25 @@
         for j in range(tiles):
             norm_buf[j, col] = value[:, j * depth:(j + 1) * depth]
 
-    normalise(tok_ref, s)
-
-    def fold_copy(k):
-        return send(
-            fold_own, fold_buf.at[lax.rem(t, share)], fold_send.at[k],
-            fold_recv.at[lax.rem(t, share)], tile_mate if k == 0 else tile_at(k), s,
-        )
+    def keep(source, col):
+        kept = jnp.dot(source[...], head_ref[...], preferred_element_type=jnp.float32)
+        kept_buf[col] = jnp.zeros(kept_buf.shape[1:], jnp.float32)
+        for q in range(groups):
+            @pl.when(s == q)
+            def _():
+                kept_buf[col, :, q * width:(q + 1) * width] = kept
+
+    own_fold = lax.rem(t, share)
+    fold_mate = send(
+        fold_own, fold_buf.at[own_fold], fold_send.at[0], fold_recv.at[own_fold], tile_mate, s
+    )
+    fold_line = {
+        step: send(
+            fold_own, fold_buf.at[own_fold], fold_send.at[(3 + step) // 2],
+            fold_recv.at[own_fold], t + 2 * step, s,
+        )
+        for step in (-1, 1)
+    }
 
     @pl.when(s == owner)
     def _():
@@ -215,65 +239,108 @@
             def _():
                 fold_own[:, q * width:(q + 1) * width] = block_in[q]
 
-        for k in range(tile_pairs):
-            fold_copy(k).start()
+        for step in (-1, 1):
+            @pl.when(line(step))
+            def _():
+                fold_line[step].start()
+        fold_mate.start()
         fold_buf[lax.rem(t, share)] = fold_own[...]
 
-    def up_forward(k):
-        at = tile_at(k)
-        return send(up_buf.at[at], up_buf.at[at], up_fsend.at[k], up_recv.at[at], tile_mate, s)
-
-    def fold_forward(j):
+    def up_forward(k, step):
+        at = t - 2 * step * k
+        return (
+            send(up_buf.at[at], up_buf.at[at], up_fsend.at[at // 2], up_recv.at[at], tile_mate, s),
+            send(up_buf.at[at], up_buf.at[at], up_lsend.at[at // 2], up_recv.at[at], t + 2 * step, s),
+        )
+
+    def fold_forward(j, step):
         at = 2 * j + side
-        return send(fold_buf.at[at], fold_buf.at[at], fold_fsend.at[j], fold_recv.at[at], tile_mate, s)
-
-    def fold_is_mine(j):
-        return pair == s * (share // 2) + j
+        return (
+            send(fold_buf.at[at], fold_buf.at[at], fold_fsend.at[j], fold_recv.at[at], tile_mate, s),
+            send(fold_buf.at[at], fold_buf.at[at], fold_lsend.at[j], fold_recv.at[at], t + 2 * step, s),
+        )
+
+    def fold_pair(j):
+        return s * (share // 2) + j
+
+    def up_handle(k, act):
+        for step in (1, -1):
+            @pl.when(line(-step * k))
+            def _():
+                act(up_forward(k, step), step)
+
+    def fold_handle(k, act):
+        for j in range(share // 2):
+            for step in (1, -1):
+                @pl.when(pair == fold_pair(j) + step * k)
+                def _():
+                    act(fold_forward(j, step), step)
+
+    def pass_on(copies, step):
+        copies[0].wait_recv()
+
+        @pl.when(line(step))
+        def _():
+            copies[1].start()
+        copies[0].start()
+
+    def finish(copies, step):
+        copies[0].wait_send()
+
+        @pl.when(line(step))
+        def _():
+            copies[1].wait_send()
 
     def tok_forward(k):
         at = col_at(k)
         return send(tok_buf.at[at], tok_buf.at[at], tok_fsend.at[k], tok_recv.at[at], t, col_mate)
 
+    def add_block(rows_ref, at, cols, first=False):
+        for g in cols:
+            value = jnp.dot(norm_buf[at, g], rows_ref[...], preferred_element_type=jnp.float32)
+            if first:
+                acc[g] = value
+            else:
+                acc[g] = acc[g] + value
+
+    near = [s, col_mate]
+    normalise(tok_ref, s)
     for k in range(1, tile_pairs):
-        up_forward(k).wait_recv()
-        up_forward(k).start()
+        up_handle(k, pass_on)
+        if k > 1:
+            fold_handle(k - 1, pass_on)
         if k == 1:
             send(
                 tok_ref, tok_buf.at[col_mate], tok_send.at[0], tok_recv.at[col_mate], t, col_mate
             ).wait_recv()
             normalise(tok_buf.at[col_mate], col_mate)
-    for j in range(share // 2):
-        @pl.when(jnp.logical_not(fold_is_mine(j)))
-        def _():
-            fold_forward(j).wait_recv()
-            fold_forward(j).start()
+            keep(tok_ref, s)
+            add_block(up_ref, t, near, True)
+    fold_handle(tile_pairs - 1, pass_on)
     for k in range(1, chips):
         tok_forward(k).wait_recv()
         tok_forward(k).start()
+    keep(tok_buf.at[col_mate], col_mate)
     for k in range(1, chips):
         normalise(tok_buf.at[col_at(k)], col_at(k))
+        keep(tok_buf.at[col_at(k)], col_at(k))
+    far = []
     for k in range(1, chips):
         at = 2 * lax.rem(chip + k, chips) + 1 - core
         send(tok_ref, tok_buf.at[at], tok_send.at[0], tok_recv.at[at], t, col_mate).wait_recv()
         normalise(tok_buf.at[at], at)
-
-    def add_block(rows_ref, at, first=False):
-        def step(g, carry):
-            value = jnp.dot(norm_buf[at, g], rows_ref[...], preferred_element_type=jnp.float32)
-            if first:
-                acc[g] = value
-            else:
-                acc[g] = acc[g] + value
-            return carry
-        lax.fori_loop(0, groups, step, 0)
-
-    add_block(up_ref, t, True)
+        keep(tok_buf.at[at], at)
+        far += [col_at(k), at]
+    add_block(up_ref, t, far, True)
     for k in range(1, tile_pairs):
-        add_block(up_buf.at[tile_at(k)], tile_at(k))
+        add_block(up_buf.at[tile_at(k)], tile_at(k), near + far)
     for k in range(tile_pairs):
-        at = 2 * lax.rem(pair + k, tile_pairs) + 1 - side
-        send(up_ref, up_buf.at[at], up_send.at[0], up_recv.at[at], tile_mate, s).wait_recv()
-        add_block(up_buf.at[at], at)
+        for step in ((1, -1) if k else (1,)):
+            @pl.when(line(-step * k))
+            def _():
+                at = tile_mate - 2 * step * k
+                send(up_ref, up_buf.at[at], up_send.at[0], up_recv.at[at], tile_mate, s).wait_recv()
+                add_block(up_buf.at[at], at, near + far)
     for j in range(share // 2):
         at = 2 * j + 1 - side
         send(fold_own, fold_buf.at[at], fold_send.at[0], fold_recv.at[at], tile_mate, s).wait_recv()
@@ -286,18 +353,9 @@
         value = acc[col]
         inner = 0.7978845608028654 * (value + 0.044715 * (value * value * value))
         hidden = (0.5 * value * (1.0 + jnp.tanh(inner))).astype(jnp.bfloat16)
-        target[...] = jnp.dot(hidden, fold_all[...], preferred_element_type=jnp.float32)
-
-        def keep(source):
-            kept = jnp.dot(source[...], head_ref[...], preferred_element_type=jnp.float32)
-            for q in range(groups):
-                @pl.when(s == q)
-                def _():
-                    target[:, q * width:(q + 1) * width] += kept
-
-        keep(tok_buf.at[col])
-
-    tok_buf[s] = tok_ref[...]
+        target[...] = (
+            jnp.dot(hidden, fold_all[...], preferred_element_type=jnp.float32) + kept_buf[col]
+        )
 
     def sib_copy(k):
         return send(part.at[k], sib_buf.at[k], sib_send.at[k], sib_recv.at[k], t, col_mate)
@@ -320,10 +378,15 @@
         total = total + cross_in[k].astype(jnp.float32)
     out_ref[...] = total.astype(jnp.bfloat16)
 
-    for copy in up_copies + tok_copies:
+    for copy in [up_mate] + tok_copies:
         copy.wait_send()
+    for step in (-1, 1):
+        @pl.when(line(step))
+        def _():
+            up_line[step].wait_send()
     for k in range(1, tile_pairs):
-        up_forward(k).wait_send()
+        up_handle(k, finish)
+        fold_handle(k, finish)
     for k in range(1, chips):
         tok_forward(k).wait_send()
         cross_copy(k).wait_send()
@@ -336,13 +399,11 @@
 
     @pl.when(s == owner)
     def _():
-        for k in range(tile_pairs):
-            fold_copy(k).wait_send()
-
-    for j in range(share // 2):
-        @pl.when(jnp.logical_not(fold_is_mine(j)))
-        def _():
-            fold_forward(j).wait_send()
+        fold_mate.wait_send()
+        for step in (-1, 1):
+            @pl.when(line(step))
+            def _():
+                fold_line[step].wait_send()
 
 
 def surrogate(tokens, gain, up, down, head, tiles, groups):
@@ -374,14 +435,15 @@
             pltpu.VMEM((chips, rows, outs), f32),
             pltpu.VMEM((chips, rows, outs), bf16),
             pltpu.VMEM((chips, rows, outs), bf16),
-            dma((tiles // 2,)), dma((tiles // 2,)), dma((tiles,)),
+            pltpu.VMEM((groups, rows, outs), f32),
+            dma((3,)), dma((tiles // 2,)), dma((tiles // 2,)), dma((tiles,)),
             dma((chips,)), dma((chips,)), dma((groups,)),
             dma(()), dma((groups,)),
-            dma((tiles // 2,)), dma((share // 2,)), dma((share,)),
+            dma((3,)), dma((share // 2,)), dma((share // 2,)), dma((share,)),
             dma((chips,)), dma((chips,)), dma((chips,)), dma((chips,)),
         ],
         compiler_params=pltpu.CompilerParams(
-            collective_id=0, has_side_effects=True, vmem_limit_bytes=52 * 1024 * 1024
+            collective_id=0, has_side_effects=True, vmem_limit_bytes=44 * 1024 * 1024
         ),
         name="surrogate_kernel",
     )(tokens, gain.reshape(1, -1), up, down, head)

time: 125 us -> 114 us (0.912)
  the two profiles are of different devices: /device:TPU:9 before, /device:TPU:1 now
where the time goes in v3:
time: 114 us
  Pallas kernels  103 us (90%)
  local copies, waits for them, and re-layouts  10.3 us (9%)
    pallas_call x1, Pallas kernels, surrogate(): pl.pallas_call(functools.partial(surrogate_kernel, tiles, groups), out_sh...  90.9 us
    pallas_call x1, Pallas kernels, image(): pl.pallas_call(functools.partial(image_kernel, sources), out_shape=jax.Sh...  12.3 us
    unnamed x22, local copies, waits for them, and re-layouts  9.26 us

profile of v3, /device:TPU:1, one launch (start us, length us, event | category | flops | bytes accessed | tf_op | source)
XLA Modules:
  0.0 113.6 jit_solution(16899412854923046544)
XLA Ops:
  0.0 0.0 copy-start
  0.0 1.4 %copy-done = bf16[256,2816]{1,0:T(8,128)(2,1)S(1)} copy-done((bf16[256,2816]{1,0:T(8,128)(2,1)S(1)}, bf16[256,2816]{1,0:T(8,128)(2,1)}, u32[]{:S(2)}) %copy-start) | copy-done | bytes 1441816
  1.4 0.2 constant_dynamic-slice_fusion
  1.6 0.0 copy-start.6
  1.6 1.4 %copy.16.head_ref = bf16[2048,192]{1,0:T(8,128)(2,1)S(1)} copy(bf16[2048,192]{0,1:T(8,128)(2,1)} %param.16) | data formatting | bytes 1572864 | tf_op args[4]
  3.1 0.0 copy-done.6
  3.1 0.0 copy-start.1
  3.1 1.4 %copy-done.1 = bf16[352,2048]{1,0:T(8,128)(2,1)S(1)} copy-done((bf16[352,2048]{1,0:T(8,128)(2,1)S(1)}, bf16[352,2048]{1,0:T(8,128)(2,1)}, u32[]{:S(2)}) %copy-start.1) | copy-done | bytes 1441816
  4.4 0.0 copy-start.2
  4.4 1.2 %copy-done.2 = bf16[256,2048]{1,0:T(8,128)(2,1)S(1)} copy-done((bf16[256,2048]{1,0:T(8,128)(2,1)S(1)}, bf16[256,2048]{1,0:T(8,128)(2,1)}, u32[]{:S(2)}) %copy-start.2) | copy-done | bytes 1048600
  5.7 0.0 copy-start.4
  5.7 0.0 copy-start.7
  5.7 90.9 %surrogate_kernel.1.coeffs_ref = bf16[256,768]{1,0:T(8,128)(2,1)S(1)} custom-call(bf16[256,2048]{1,0:T(8,128)(2,1)S(1)} %copy-done.2, f32[1,2048]{1,0:T(1,128)S(1)} %bitcast.1, bf16[256,768]{1,0:T(8,128)(2,1)S(1)} %pad.4.up_ref, bf16[352,2048]{1,0:T(8,128)(2,1)S(1)} %copy-done.1, bf16[2048,192]{1,0:T(8,128)(2,1)S(1)} %copy.16.head_ref), custom_call_target="tpu_custom_call" | custom-call | tf_op jit(solution)/shard_map/surrogate_kernel/pallas_call | solution.py:418
  96.6 0.8 copy.15
  97.4 0.1 reshape.9.index_ref
  97.5 0.0 copy-done.4
  97.5 0.0 copy-done.7
  97.5 0.0 copy-start.3
  97.5 1.0 copy-done.3
  98.5 0.8 copy-done.5
  99.3 0.7 copy-done.8
  99.9 0.7 copy-done.9
  100.6 12.3 %image_kernel.1 = f32[64,64]{1,0:T(8,128)S(1)} custom-call(s32[64]{0:T(128)S(1)} %reshape.9.index_ref, s32[32]{0:T(128)S(1)} %copy-done.8, f32[32]{0:T(128)S(1)} %copy-done.9, bf16[256,768]{1,0:T(8,128)(2,1)S(1)} %surrogate_kernel.1.coeffs_ref, bf16[128,2048]{1,0:T(8,128)(2,1)S(1)} %copy-done.3, bf16[16,256]{1,0:T(8,128)(2,1)S(1)} %copy-done.7, ...), custom_call_target="tpu_custom_call" | custom-call | tf_op jit(solution)/shard_map/image_kernel/pallas_call | solution.py:113
  112.9 0.7 reshape.11
  (4 shorter events, 0.0 us)
Async XLA Ops:
  0.0 1.4 %copy-start = (bf16[256,2816]{1,0:T(8,128)(2,1)S(1)}, bf16[256,2816]{1,0:T(8,128)(2,1)}, u32[]{:S(2)}) copy-start(bf16[256,2816]{1,0:T(8,128)(2,1)} %param.14) | copy-start | bytes 4325380
  1.6 1.5 %copy-start.6 = (f32[2048]{0:T(1024)S(1)}, f32[2048]{0:T(1024)}, u32[]{:S(2)}) copy-start(f32[2048]{0:T(1024)} %param.13) | copy-start | bytes 24580
  3.1 1.4 %copy-start.1 = (bf16[352,2048]{1,0:T(8,128)(2,1)S(1)}, bf16[352,2048]{1,0:T(8,128)(2,1)}, u32[]{:S(2)}) copy-start(bf16[352,2048]{1,0:T(8,128)(2,1)} %down_ref.1) | copy-start | bytes 4325380
  4.4 1.2 %copy-start.2 = (bf16[256,2048]{1,0:T(8,128)(2,1)S(1)}, bf16[256,2048]{1,0:T(8,128)(2,1)}, u32[]{:S(2)}) copy-start(bf16[256,2048]{1,0:T(8,128)(2,1)} %tok_ref.1) | copy-start | bytes 3145732
  5.7 91.8 %copy-start.4 = (bf16[256,512]{1,0:T(8,128)(2,1)S(1)}, bf16[256,512]{1,0:T(8,128)(2,1)}, u32[]{:S(2)}) copy-start(bf16[256,512]{1,0:T(8,128)(2,1)} %constant.22.clone.one_ref) | copy-start | bytes 786436
  5.7 91.8 %copy-start.7 = (bf16[16,256]{1,0:T(8,128)(2,1)S(1)}, bf16[16,256]{1,0:T(8,128)(2,1)}, u32[]{:S(2)}) copy-start(bf16[16,256]{1,0:T(8,128)(2,1)} %constant.21.clone.gather_ref) | copy-start | bytes 24580
  97.5 1.0 copy-start.3
  98.5 0.8 copy-start.5
  99.3 0.7 copy-start.8
  99.9 0.7 copy-start.9

commit v4 on v3

--- a/solution.py
+++ b/solution.py
@@ -32,29 +32,28 @@
     angle = 2 * np.pi * (np.outer(np.arange(PIX), np.arange(W)) % PIX) / PIX
     high, low = split_two(np.concatenate([np.cos(angle), np.sin(angle)], 1))
     table_two = np.concatenate([high, low, high], 1)
-    spread = np.zeros((2 * SUB, SUB, 2 * SUB, GRID, SUB), ml_dtypes.bfloat16)
-    for cu in range(2 * SUB):
-        for v in range(SUB):
-            spread[cu, v, cu, :, v] = 1
-    spread = spread.reshape(2 * SUB * SUB, 2 * SUB * ORD)
-    gather = np.repeat(np.eye(GRID), GRID, 1).astype(ml_dtypes.bfloat16)
-    return spread, gather, table_one, table_two
+    return table_one, table_two
 
 
 def image_kernel(
-    sources, index_ref, cutoff_ref, weight_ref, coeffs_ref, spread_ref, gather_ref,
-    one_ref, two_ref, out_ref, spectra,
+    sources, index_ref, cutoff_ref, weight_ref, coeffs_ref, one_ref, two_ref, out_ref, spectra,
 ):
     row = lax.broadcasted_iota(jnp.int32, (PATCH, 2 * SUB * ORD), 0)
     lane = lax.broadcasted_iota(jnp.int32, (PATCH, 2 * SUB * ORD), 1)
     own = (row % GRID) == ((lane % ORD) // SUB)
+    row, lane = row[:128], lane[:128]
+    same = (row // SUB == lane // ORD) & (row % SUB == lane % SUB)
+    spread = jnp.where(same, 1.0, 0.0).astype(jnp.bfloat16)
+    row = lax.broadcasted_iota(jnp.int32, (GRID, PATCH), 0)
+    lane = lax.broadcasted_iota(jnp.int32, (GRID, PATCH), 1)
+    gather = jnp.where(row == lane // GRID, 1.0, 0.0).astype(jnp.bfloat16)
     for pair in range(6):
         wide = jnp.dot(
-            coeffs_ref[:, pair * 128:(pair + 1) * 128], spread_ref[...],
+            coeffs_ref[:, pair * 128:(pair + 1) * 128], spread,
             preferred_element_type=jnp.float32,
         )
         kept = jnp.where(own, wide, 0.0).astype(jnp.bfloat16)
-        rows = jnp.dot(gather_ref[...], kept, preferred_element_type=jnp.float32)
+        rows = jnp.dot(gather, kept, preferred_element_type=jnp.float32)
         for part in range(2):
             for u in range(SUB):
                 at = (part * SUB + u) * ORD
@@ -101,7 +100,7 @@
             power = power + field[:, k * 128:(k + 1) * 128]
         return total + weight_ref[s] * power
 
-    total = lax.fori_loop(0, sources, add_source, jnp.zeros((PIX, 128), jnp.float32), unroll=4)
+    total = lax.fori_loop(0, sources, add_source, jnp.zeros((PIX, 128), jnp.float32), unroll=8)
     out_ref[...] = (total[:, :PIX] + total[:, PIX:]) * (1.0 / (6.0 * W * W * sources))
 
 
@@ -113,7 +112,7 @@
     out = pl.pallas_call(
         functools.partial(image_kernel, sources),
         out_shape=jax.ShapeDtypeStruct((PIX, PIX), jnp.float32),
-        in_specs=[smem] * 3 + [vmem] * 5,
+        in_specs=[smem] * 3 + [vmem] * 3,
         out_specs=vmem,
         scratch_shapes=[pltpu.VMEM((12, ORD, ORD), jnp.float32)],
         compiler_params=pltpu.CompilerParams(vmem_limit_bytes=24 * 1024 * 1024),

time: 114 us -> 110 us (0.965)
  local copies, waits for them, and re-layouts: 10.3 us -> 7.94 us
    unnamed x22 -> x18, local copies, waits for them, and re-layouts: 9.26 us -> 6.91 us
    pallas_call x1, Pallas kernels: 12.3 us -> 11 us  [image(): pl.pallas_call(functools.partial(image_kernel, sources), out_shape=jax.Sh...]
where the time goes in v4:
time: 110 us
  Pallas kernels  102 us (93%)
  local copies, waits for them, and re-layouts  7.94 us (7%)
    pallas_call x1, Pallas kernels, surrogate(): pl.pallas_call(functools.partial(surrogate_kernel, tiles, groups), out_sh...  90.9 us
    pallas_call x1, Pallas kernels, image(): pl.pallas_call(functools.partial(image_kernel, sources), out_shape=jax.Sh...  11 us
    unnamed x18, local copies, waits for them, and re-layouts  6.91 us

profile of v4, /device:TPU:1, one launch (start us, length us, event | category | flops | bytes accessed | tf_op | source)
XLA Modules:
  0.0 110.0 jit_solution(821248537144181707)
XLA Ops:
  0.0 0.0 copy-start
  0.0 1.4 %copy-done = bf16[256,2816]{1,0:T(8,128)(2,1)S(1)} copy-done((bf16[256,2816]{1,0:T(8,128)(2,1)S(1)}, bf16[256,2816]{1,0:T(8,128)(2,1)}, u32[]{:S(2)}) %copy-start) | copy-done | bytes 1441816
  1.4 0.2 constant_dynamic-slice_fusion
  1.6 0.0 copy-start.5
  1.6 1.4 %copy.14.head_ref = bf16[2048,192]{1,0:T(8,128)(2,1)S(1)} copy(bf16[2048,192]{0,1:T(8,128)(2,1)} %param.14) | data formatting | bytes 1572864 | tf_op args[4]
  3.1 0.0 copy-done.5
  3.1 0.0 copy-start.1
  3.1 1.4 %copy-done.1 = bf16[352,2048]{1,0:T(8,128)(2,1)S(1)} copy-done((bf16[352,2048]{1,0:T(8,128)(2,1)S(1)}, bf16[352,2048]{1,0:T(8,128)(2,1)}, u32[]{:S(2)}) %copy-start.1) | copy-done | bytes 1441816
  4.4 0.0 copy-start.2
  4.4 1.2 %copy-done.2 = bf16[256,2048]{1,0:T(8,128)(2,1)S(1)} copy-done((bf16[256,2048]{1,0:T(8,128)(2,1)S(1)}, bf16[256,2048]{1,0:T(8,128)(2,1)}, u32[]{:S(2)}) %copy-start.2) | copy-done | bytes 1048600
  5.7 0.0 copy-start.3
  5.7 0.0 copy-start.6
  5.7 0.0 copy-start.7
  5.7 90.9 %surrogate_kernel.1.coeffs_ref = bf16[256,768]{1,0:T(8,128)(2,1)S(1)} custom-call(bf16[256,2048]{1,0:T(8,128)(2,1)S(1)} %copy-done.2, f32[1,2048]{1,0:T(1,128)S(1)} %bitcast.1, bf16[256,768]{1,0:T(8,128)(2,1)S(1)} %pad.4.up_ref, bf16[352,2048]{1,0:T(8,128)(2,1)S(1)} %copy-done.1, bf16[2048,192]{1,0:T(8,128)(2,1)S(1)} %copy.14.head_ref), custom_call_target="tpu_custom_call" | custom-call | tf_op jit(solution)/shard_map/surrogate_kernel/pallas_call | solution.py:417
  96.6 0.8 copy.13
  97.4 0.1 reshape.9.index_ref
  97.5 0.0 copy-done.3
  97.5 0.0 copy-done.6
  97.5 0.0 copy-done.7
  97.5 0.0 copy-start.4
  97.5 0.7 copy-done.4
  98.3 11.0 %image_kernel.1 = f32[64,64]{1,0:T(8,128)S(1)} custom-call(s32[64]{0:T(128)S(1)} %reshape.9.index_ref, s32[32]{0:T(128)S(1)} %copy-done.6, f32[32]{0:T(128)S(1)} %copy-done.7, bf16[256,768]{1,0:T(8,128)(2,1)S(1)} %surrogate_kernel.1.coeffs_ref, bf16[256,512]{1,0:T(8,128)(2,1)S(1)} %copy-done.3, bf16[64,192]{1,0:T(8,128)(2,1)S(1)} %copy-done.4), custom_call_target="tpu_custom_call" | custom-call | tf_op jit(solution)/shard_map/image_kernel/pallas_call | solution.py:112
  109.3 0.7 reshape.11
  (1 shorter events, 0.0 us)
Async XLA Ops:
  0.0 1.4 %copy-start = (bf16[256,2816]{1,0:T(8,128)(2,1)S(1)}, bf16[256,2816]{1,0:T(8,128)(2,1)}, u32[]{:S(2)}) copy-start(bf16[256,2816]{1,0:T(8,128)(2,1)} %param.12) | copy-start | bytes 4325380
  1.6 1.5 %copy-start.5 = (f32[2048]{0:T(1024)S(1)}, f32[2048]{0:T(1024)}, u32[]{:S(2)}) copy-start(f32[2048]{0:T(1024)} %param.11) | copy-start | bytes 24580
  3.1 1.4 %copy-start.1 = (bf16[352,2048]{1,0:T(8,128)(2,1)S(1)}, bf16[352,2048]{1,0:T(8,128)(2,1)}, u32[]{:S(2)}) copy-start(bf16[352,2048]{1,0:T(8,128)(2,1)} %down_ref.1) | copy-start | bytes 4325380
  4.4 1.2 %copy-start.2 = (bf16[256,2048]{1,0:T(8,128)(2,1)S(1)}, bf16[256,2048]{1,0:T(8,128)(2,1)}, u32[]{:S(2)}) copy-start(bf16[256,2048]{1,0:T(8,128)(2,1)} %tok_ref.1) | copy-start | bytes 3145732
  5.7 91.8 %copy-start.3 = (bf16[256,512]{1,0:T(8,128)(2,1)S(1)}, bf16[256,512]{1,0:T(8,128)(2,1)}, u32[]{:S(2)}) copy-start(bf16[256,512]{1,0:T(8,128)(2,1)} %constant.16.clone.one_ref) | copy-start | bytes 786436
  5.7 91.8 %copy-start.6 = (s32[32]{0:T(128)S(1)}, s32[32]{0:T(128)}, u32[]{:S(2)}) copy-start(s32[32]{0:T(128)} %cutoff_ref.1) | copy-start | bytes 388
  5.7 91.8 %copy-start.7 = (f32[32]{0:T(128)S(1)}, f32[32]{0:T(128)}, u32[]{:S(2)}) copy-start(f32[32]{0:T(128)} %weight_ref.1) | copy-start | bytes 388
  97.5 0.8 copy-start.4

commit v5 on v4

--- a/solution.py
+++ b/solution.py
@@ -63,8 +63,8 @@
     order_j = lax.broadcasted_iota(jnp.int32, (W, ORD), 1) - W // 2
 
     def add_source(s, total):
-        x0 = index_ref[2 * s]
-        y0 = index_ref[2 * s + 1]
+        x0 = index_ref[s, 0]
+        y0 = index_ref[s, 1]
         radius = cutoff_ref[s]
         col = order_j - y0
         inside = (order_i * order_i + col * col <= radius * radius) & (col < W // 2)
@@ -101,7 +101,9 @@
         return total + weight_ref[s] * power
 
     total = lax.fori_loop(0, sources, add_source, jnp.zeros((PIX, 128), jnp.float32), unroll=8)
-    out_ref[...] = (total[:, :PIX] + total[:, PIX:]) * (1.0 / (6.0 * W * W * sources))
+    total = (total[:, :PIX] + total[:, PIX:]) * (1.0 / (6.0 * W * W * sources))
+    for x in range(0, PIX, 2):
+        out_ref[:, x * PIX:(x + 2) * PIX] = jnp.concatenate([total[x:x + 1], total[x + 1:x + 2]], 1)
 
 
 def image(coeffs, source_index, source_cutoff, source_weight):
@@ -109,16 +111,15 @@
     smem = pl.BlockSpec(memory_space=pltpu.SMEM)
     vmem = pl.BlockSpec(memory_space=pltpu.VMEM)
     tables = [jnp.asarray(t) for t in image_tables()]
-    out = pl.pallas_call(
+    return pl.pallas_call(
         functools.partial(image_kernel, sources),
-        out_shape=jax.ShapeDtypeStruct((PIX, PIX), jnp.float32),
+        out_shape=jax.ShapeDtypeStruct((1, PIX * PIX), jnp.float32),
         in_specs=[smem] * 3 + [vmem] * 3,
         out_specs=vmem,
         scratch_shapes=[pltpu.VMEM((12, ORD, ORD), jnp.float32)],
         compiler_params=pltpu.CompilerParams(vmem_limit_bytes=24 * 1024 * 1024),
         name="image_kernel",
-    )(source_index.reshape(-1), source_cutoff, source_weight, coeffs, *tables)
-    return out.reshape(1, PIX * PIX)
+    )(source_index, source_cutoff, source_weight, coeffs, *tables)
 
 
 MESH = pl.DeviceIdType.MESH

time: 110 us -> 110 us (level)
  no operation moved by 1% of the time
where the time goes in v5:
time: 110 us
  Pallas kernels  103 us (94%)
  local copies, waits for them, and re-layouts  7.15 us (6%)
    pallas_call x1, Pallas kernels, surrogate(): pl.pallas_call(functools.partial(surrogate_kernel, tiles, groups), out_sh...  90.9 us
    pallas_call x1, Pallas kernels, image(): pl.pallas_call(functools.partial(image_kernel, sources), out_shape=jax.Sh...  12 us
    unnamed x18, local copies, waits for them, and re-layouts  6.91 us

profile of v5, /device:TPU:1, one launch (start us, length us, event | category | flops | bytes accessed | tf_op | source)
XLA Modules:
  0.0 110.1 jit_solution(6731605385017837541)
XLA Ops:
  0.0 0.0 copy-start
  0.0 1.4 %copy-done = bf16[256,2816]{1,0:T(8,128)(2,1)S(1)} copy-done((bf16[256,2816]{1,0:T(8,128)(2,1)S(1)}, bf16[256,2816]{1,0:T(8,128)(2,1)}, u32[]{:S(2)}) %copy-start) | copy-done | bytes 1441816
  1.4 0.2 constant_dynamic-slice_fusion
  1.6 0.0 copy-start.5
  1.6 1.4 %copy.11.head_ref = bf16[2048,192]{1,0:T(8,128)(2,1)S(1)} copy(bf16[2048,192]{0,1:T(8,128)(2,1)} %param.14) | data formatting | bytes 1572864 | tf_op args[4]
  3.1 0.0 copy-done.5
  3.1 0.0 copy-start.1
  3.1 1.4 %copy-done.1 = bf16[352,2048]{1,0:T(8,128)(2,1)S(1)} copy-done((bf16[352,2048]{1,0:T(8,128)(2,1)S(1)}, bf16[352,2048]{1,0:T(8,128)(2,1)}, u32[]{:S(2)}) %copy-start.1) | copy-done | bytes 1441816
  4.4 0.0 copy-start.2
  4.4 1.2 %copy-done.2 = bf16[256,2048]{1,0:T(8,128)(2,1)S(1)} copy-done((bf16[256,2048]{1,0:T(8,128)(2,1)S(1)}, bf16[256,2048]{1,0:T(8,128)(2,1)}, u32[]{:S(2)}) %copy-start.2) | copy-done | bytes 1048600
  5.7 0.0 copy-start.3
  5.7 0.0 copy-start.6
  5.7 0.0 copy-start.7
  5.7 90.9 %surrogate_kernel.1.coeffs_ref = bf16[256,768]{1,0:T(8,128)(2,1)S(1)} custom-call(bf16[256,2048]{1,0:T(8,128)(2,1)S(1)} %copy-done.2, f32[1,2048]{1,0:T(1,128)S(1)} %bitcast.1, bf16[256,768]{1,0:T(8,128)(2,1)S(1)} %pad.4.up_ref, bf16[352,2048]{1,0:T(8,128)(2,1)S(1)} %copy-done.1, bf16[2048,192]{1,0:T(8,128)(2,1)S(1)} %copy.11.head_ref), custom_call_target="tpu_custom_call" | custom-call | tf_op jit(solution)/shard_map/surrogate_kernel/pallas_call | solution.py:418
  96.6 0.8 copy.12.index_ref
  97.4 0.0 copy-done.3
  97.4 0.0 copy-done.6
  97.4 0.0 copy-done.7
  97.4 0.0 copy-start.4
  97.4 0.7 copy-done.4
  98.1 12.0 %image_kernel.1 = f32[1,4096]{1,0:T(1,128)} custom-call(s32[32,2]{1,0:T(8,128)S(1)} %copy.12.index_ref, s32[32]{0:T(128)S(1)} %copy-done.6, f32[32]{0:T(128)S(1)} %copy-done.7, bf16[256,768]{1,0:T(8,128)(2,1)S(1)} %surrogate_kernel.1.coeffs_ref, bf16[256,512]{1,0:T(8,128)(2,1)S(1)} %copy-done.3, bf16[64,192]{1,0:T(8,128)(2,1)S(1)} %copy-done.4), custom_call_target="tpu_custom_call" | custom-call | tf_op jit(solution)/shard_map/image_kernel/pallas_call | solution.py:114
  (1 shorter events, 0.0 us)
Async XLA Ops:
  0.0 1.4 %copy-start = (bf16[256,2816]{1,0:T(8,128)(2,1)S(1)}, bf16[256,2816]{1,0:T(8,128)(2,1)}, u32[]{:S(2)}) copy-start(bf16[256,2816]{1,0:T(8,128)(2,1)} %param.12) | copy-start | bytes 4325380
  1.6 1.5 %copy-start.5 = (f32[2048]{0:T(1024)S(1)}, f32[2048]{0:T(1024)}, u32[]{:S(2)}) copy-start(f32[2048]{0:T(1024)} %param.11) | copy-start | bytes 24580
  3.1 1.4 %copy-start.1 = (bf16[352,2048]{1,0:T(8,128)(2,1)S(1)}, bf16[352,2048]{1,0:T(8,128)(2,1)}, u32[]{:S(2)}) copy-start(bf16[352,2048]{1,0:T(8,128)(2,1)} %down_ref.1) | copy-start | bytes 4325380
  4.4 1.2 %copy-start.2 = (bf16[256,2048]{1,0:T(8,128)(2,1)S(1)}, bf16[256,2048]{1,0:T(8,128)(2,1)}, u32[]{:S(2)}) copy-start(bf16[256,2048]{1,0:T(8,128)(2,1)} %tok_ref.1) | copy-start | bytes 3145732
  5.7 91.7 %copy-start.3 = (bf16[256,512]{1,0:T(8,128)(2,1)S(1)}, bf16[256,512]{1,0:T(8,128)(2,1)}, u32[]{:S(2)}) copy-start(bf16[256,512]{1,0:T(8,128)(2,1)} %constant.16.clone.one_ref) | copy-start | bytes 786436
  5.7 91.7 %copy-start.6 = (s32[32]{0:T(128)S(1)}, s32[32]{0:T(128)}, u32[]{:S(2)}) copy-start(s32[32]{0:T(128)} %cutoff_ref.1) | copy-start | bytes 388
  5.7 91.7 %copy-start.7 = (f32[32]{0:T(128)S(1)}, f32[32]{0:T(128)}, u32[]{:S(2)}) copy-start(f32[32]{0:T(128)} %weight_ref.1) | copy-start | bytes 388
  97.4 0.8 copy-start.4
